TPU v7x, 256 devices: a whole 4x4x8 slice. The times are simulated.
256 devices in a mesh: seq: 128 (over y_hi, x, z, core), chan: 2 (over y_lo).
Axes of the slice: x: 4, y: 4 (y_hi: 2, y_lo: 2; y = y_hi * 2 + y_lo), z: 8, core: 2. Of those that a mesh axis runs over, the one named last changes fastest.
Arguments:
- inputs: bfloat16 [32768, 2048], P(('seq', 'chan')), may hold values from -6 to 6
- cotangent: bfloat16 [32768, 2048], P(('seq', 'chan')), may hold values from -6 to 6
- filter_spec: bfloat16 [2, 256, 128, 2048], P(None, 'seq', None, 'chan'), may hold values from -6 to 6
Outputs:
- grad_input: bfloat16 [32768, 2048], P(('seq', 'chan'))
- grad_filter: bfloat16 [2, 256, 128, 2048], P(None, 'seq', None, 'chan')
All inputs are finite; a program needn't handle non-finite values.
Results may differ from a plain program's by a relative error of at most 0.001.
Values may be sent and summed in bfloat16 or wider, within the bound.
A program may use at most 128 MiB of HBM per device.

v0:
```python
import math

import jax
import jax.numpy as jnp
from jax import lax
from jax.sharding import PartitionSpec as P

exact_mode = lax.Precision.HIGHEST
full_turn = 2.0 * math.pi


def class_of(slot_ids, slot_count):
    halved = slot_ids // 2
    return jnp.where(
        slot_ids % 2 == 0, halved, jnp.where(slot_ids == 1, slot_count // 2, slot_count - halved)
    )


def angle_table(numerator, modulus):
    reduced = (numerator % modulus).astype(jnp.float32) * (full_turn / modulus)
    return (jnp.cos(reduced), -jnp.sin(reduced))


def token_offset(position, own_count, per_peer, tok_count):
    source = position // own_count
    within = position % own_count
    return within // per_peer * tok_count + source * per_peer + within % per_peer


def matmul_exact(left, right):
    return jnp.dot(left, right, precision=exact_mode, preferred_element_type=jnp.float32)


def einsum_exact(form, left, right):
    return jnp.einsum(form, left, right, precision=exact_mode, preferred_element_type=jnp.float32)


def rotate(real_part, imag_part, cos_part, sin_part):
    return (
        real_part * cos_part - imag_part * sin_part,
        real_part * sin_part + imag_part * cos_part,
    )


def mirror(values, first_device):
    generic = values[::-1, ::-1]
    special = jnp.stack([jnp.roll(values[0, ::-1], 1, axis=0), values[1, ::-1]])
    return jnp.where(first_device, special, generic)


def local(inputs, cotangent, filter_spec):
    tok_count, full_width = inputs.shape
    shard_count = lax.axis_size("seq")
    group_count = lax.axis_size("chan")
    per_peer = tok_count // shard_count
    own_count = group_count * per_peer
    block_size = tok_count * group_count
    half_block = block_size // 2
    slot_count = 2 * shard_count
    points = slot_count * block_size
    group_width = full_width // group_count
    shard_index = lax.axis_index("seq")
    first_device = shard_index == 0
    got_inputs, got_cotangent = (
        lax.all_to_all(
            lax.all_to_all(
                inputs.reshape(1, 1, tok_count, full_width),
                "seq",
                split_axis=2,
                concat_axis=0,
                tiled=True,
            ),
            "chan",
            split_axis=3,
            concat_axis=1,
            tiled=True,
        ),
        lax.all_to_all(
            lax.all_to_all(
                cotangent.reshape(1, 1, tok_count, full_width),
                "seq",
                split_axis=2,
                concat_axis=0,
                tiled=True,
            ),
            "chan",
            split_axis=3,
            concat_axis=1,
            tiled=True,
        ),
    )
    rows_input = got_inputs.reshape(shard_count, own_count * group_width).astype(jnp.float32)
    rows_cotangent = got_cotangent.reshape(shard_count, own_count * group_width).astype(jnp.float32)
    classes = class_of(jnp.arange(slot_count, dtype=jnp.int32), slot_count)
    seq_ids = jnp.arange(shard_count, dtype=jnp.int32)
    class_cos, class_sin = angle_table(classes[:, None] * seq_ids[None, :], slot_count)
    own_offsets = token_offset(
        shard_index * own_count + jnp.arange(own_count, dtype=jnp.int32),
        own_count,
        per_peer,
        tok_count,
    )
    twist_cos, twist_sin = angle_table(classes[:, None] * own_offsets[None, :], points)
    twist_cos = twist_cos[:, :, None]
    twist_sin = twist_sin[:, :, None]
    all_offsets = token_offset(
        jnp.arange(block_size, dtype=jnp.int32), own_count, per_peer, tok_count
    )
    freq_ids = jnp.arange(block_size, dtype=jnp.int32)
    block_cos, block_sin = angle_table(freq_ids[:, None] * all_offsets[None, :], block_size)
    sectioned = (slot_count, own_count, group_width)
    input_real, input_imag = rotate(
        matmul_exact(class_cos, rows_input).reshape(sectioned),
        matmul_exact(class_sin, rows_input).reshape(sectioned),
        twist_cos,
        twist_sin,
    )
    cotan_real, cotan_imag = rotate(
        matmul_exact(class_cos, rows_cotangent).reshape(sectioned),
        matmul_exact(class_sin, rows_cotangent).reshape(sectioned),
        twist_cos,
        twist_sin,
    )
    pieces = (
        lax.all_to_all(input_real, "seq", split_axis=0, concat_axis=1, tiled=True),
        lax.all_to_all(input_imag, "seq", split_axis=0, concat_axis=1, tiled=True),
        lax.all_to_all(cotan_real, "seq", split_axis=0, concat_axis=1, tiled=True),
        lax.all_to_all(cotan_imag, "seq", split_axis=0, concat_axis=1, tiled=True),
    )
    results = []
    for member in range(0, len(pieces), 2):
        real_part = pieces[member]
        imag_part = pieces[member + 1]
        results.append(
            einsum_exact("rj,sjc->src", block_cos, real_part)
            - einsum_exact("rj,sjc->src", block_sin, imag_part)
        )
        results.append(
            einsum_exact("rj,sjc->src", block_cos, imag_part)
            + einsum_exact("rj,sjc->src", block_sin, real_part)
        )
    spec_in_real, spec_in_imag, spec_ct_real, spec_ct_imag = tuple(results)
    filter_real = filter_spec[0].astype(jnp.float32)
    filter_imag = filter_spec[1].astype(jnp.float32)
    slot_grid = lax.broadcasted_iota(jnp.int32, (2, half_block, 1), 0)
    row_grid = lax.broadcasted_iota(jnp.int32, (2, half_block, 1), 1)
    at_corner = (slot_grid == 0) & (row_grid == 0) & first_device
    upper_real = jnp.where(at_corner, filter_imag[0:1, 0:1], mirror(filter_real, first_device))
    upper_imag = jnp.where(at_corner, 0.0, -mirror(filter_imag, first_device))
    lower_imag = jnp.where(at_corner, 0.0, filter_imag)
    whole_real = jnp.concatenate([filter_real, upper_real], axis=1)
    whole_imag = jnp.concatenate([lower_imag, upper_imag], axis=1)
    weighted_real = whole_real * spec_ct_real + whole_imag * spec_ct_imag
    weighted_imag = whole_real * spec_ct_imag - whole_imag * spec_ct_real
    cross_real = spec_in_real * spec_ct_real + spec_in_imag * spec_ct_imag
    cross_imag = (spec_in_imag * spec_ct_real - spec_in_real * spec_ct_imag)[:, :half_block]
    cross_lower = cross_real[:, :half_block]
    grad_real = jnp.where(at_corner, cross_lower / points, 2.0 / points * cross_lower)
    grad_imag = jnp.where(
        at_corner,
        cross_real[0:1, half_block : half_block + 1] / points,
        -(2.0 / points) * cross_imag,
    )
    grad_filter = jnp.stack([grad_real, grad_imag]).astype(jnp.bfloat16)
    back_cos = block_cos.T
    back_sin = -block_sin.T
    before_real = einsum_exact("jr,src->sjc", back_cos, weighted_real) - einsum_exact(
        "jr,src->sjc", back_sin, weighted_imag
    )
    before_imag = einsum_exact("jr,src->sjc", back_cos, weighted_imag) + einsum_exact(
        "jr,src->sjc", back_sin, weighted_real
    )
    own_classes = class_of(2 * shard_index + jnp.arange(2, dtype=jnp.int32), slot_count)
    turn_cos, turn_sin = angle_table(own_classes[:, None] * all_offsets[None, :], points)
    back_real, back_imag = rotate(
        before_real, before_imag, turn_cos[:, :, None], -turn_sin[:, :, None]
    )
    final_cos, final_sin = angle_table(seq_ids[:, None] * classes[None, :], slot_count)
    pieces = (
        lax.all_to_all(back_real, "seq", split_axis=1, concat_axis=0, tiled=True),
        lax.all_to_all(back_imag, "seq", split_axis=1, concat_axis=0, tiled=True),
    )
    total = einsum_exact("pg,gjc->pjc", final_cos, pieces[0]) + einsum_exact(
        "pg,gjc->pjc", final_sin, pieces[1]
    )
    spatial = (total / points).astype(jnp.bfloat16)
    spatial = spatial.reshape(shard_count, group_count, per_peer, group_width)
    returned = lax.all_to_all(
        lax.all_to_all(spatial, "seq", split_axis=0, concat_axis=2, tiled=True),
        "chan",
        split_axis=1,
        concat_axis=3,
        tiled=True,
    )
    grad_input = returned.reshape(tok_count, full_width)
    return (grad_input, grad_filter)


def solution(mesh):
    return jax.shard_map(
        local,
        mesh=mesh,
        in_specs=(P(("seq", "chan"), None), P(("seq", "chan"), None), P(None, "seq", None, "chan")),
        out_specs=(P(("seq", "chan"), None), P(None, "seq", None, "chan")),
        check_vma=False,
    )
```

profile of v0, /device:TPU:1, one launch (start us, length us, event | category | flops | bytes accessed | tf_op | source)
XLA Modules:
  0.0 613.4 jit_solution(9238314583780619364)
XLA Ops:
  7.8 16.4 %all-to-all-start = ((bf16[128,2,1024]{2,1,0:T(2,128)(2,1)}), bf16[128,2,1024]{2,1,0:T(2,128)(2,1)S(1)}, u32[]{:S(2)}, u32[]{:S(2)}) async-start(bf16[128,2,1024]{2,1,0:T(2,128)(2,1)} %reshape.357), calls=%async_computation | async-start | bytes 1048576 | tf_op jit(solution)/shard_map/all_to_all | solution.py:79
  29.8 14.3 %all-to-all-done = bf16[128,2,1024]{2,1,0:T(2,128)(2,1)S(1)} async-done(((bf16[128,2,1024]{2,1,0:T(2,128)(2,1)}), bf16[128,2,1024]{2,1,0:T(2,128)(2,1)S(1)}, u32[]{:S(2)}, u32[]{:S(2)}) %all-to-all-start) | async-done | bytes 524320 | tf_op jit(solution)/shard_map/all_to_all | solution.py:79
  44.2 6.8 %all-to-all-start.8 = ((bf16[128,2,1024]{2,1,0:T(2,128)(2,1)}), bf16[128,2,1024]{2,1,0:T(2,128)(2,1)S(1)}, u32[]{:S(2)}, u32[]{:S(2)}) async-start(bf16[128,2,1024]{2,1,0:T(2,128)(2,1)} %reshape.361), calls=%async_computation.8 | async-start | bytes 1048576 | tf_op jit(solution)/shard_map/all_to_all | solution.py:66
  52.6 11.4 %reduce.3 = bf16[2048,128]{1,0:T(8,128)(2,1)S(1)} reduce(bf16[2048,1,1,128]{3,2,1,0:T(2,128)(2,1)S(1)} %bitcast.188, bf16[]{:T(256)} %broadcast.740), dimensions={1,2}, to_apply=%bitcast.132.reduce_sub_computation | reduce | bytes 1048578
  64.9 6.1 all-to-all-done.8
  76.2 11.4 %reduce.1 = bf16[2048,128]{1,0:T(8,128)(2,1)S(1)} reduce(bf16[2048,1,1,128]{3,2,1,0:T(2,128)(2,1)S(1)} %bitcast.187, bf16[]{:T(256)} %broadcast.740), dimensions={1,2}, to_apply=%bitcast.136.reduce_sub_computation | reduce | bytes 1048578
  111.2 8.7 %all-to-all-start.11 = ((f32[256,2,1024]{2,1,0:T(2,128)}), f32[256,2,1024]{2,1,0:T(2,128)S(1)}, u32[]{:S(2)}, u32[]{:S(2)}) async-start(f32[256,2,1024]{2,1,0:T(2,128)} %copy.80), calls=%async_computation.11 | async-start | bytes 4194304 | tf_op jit(solution)/shard_map/all_to_all | solution.py:126
  124.6 47.7 %all-to-all-done.11 = f32[256,2,1024]{2,1,0:T(2,128)S(1)} async-done(((f32[256,2,1024]{2,1,0:T(2,128)}), f32[256,2,1024]{2,1,0:T(2,128)S(1)}, u32[]{:S(2)}, u32[]{:S(2)}) %all-to-all-start.11) | async-done | bytes 2097184 | tf_op jit(solution)/shard_map/all_to_all | solution.py:126
  172.3 8.6 %all-to-all-start.10 = ((f32[256,2,1024]{2,1,0:T(2,128)}), f32[256,2,1024]{2,1,0:T(2,128)}, u32[]{:S(2)}, u32[]{:S(2)}) async-start(f32[256,2,1024]{2,1,0:T(2,128)} %copy.78), calls=%async_computation.10 | async-start | bytes 4194304 | tf_op jit(solution)/shard_map/all_to_all | solution.py:125
  185.6 47.4 %all-to-all-done.10 = f32[256,2,1024]{2,1,0:T(2,128)} async-done(((f32[256,2,1024]{2,1,0:T(2,128)}), f32[256,2,1024]{2,1,0:T(2,128)}, u32[]{:S(2)}, u32[]{:S(2)}) %all-to-all-start.10) | async-done | bytes 2097184 | tf_op jit(solution)/shard_map/all_to_all | solution.py:125
  233.0 8.6 %all-to-all-start.2 = ((f32[256,2,1024]{2,1,0:T(2,128)}), f32[256,2,1024]{2,1,0:T(2,128)}, u32[]{:S(2)}, u32[]{:S(2)}) async-start(f32[256,2,1024]{2,1,0:T(2,128)} %copy.59), calls=%async_computation.2 | async-start | bytes 4194304 | tf_op jit(solution)/shard_map/all_to_all | solution.py:127
  246.2 47.4 %all-to-all-done.2 = f32[256,2,1024]{2,1,0:T(2,128)} async-done(((f32[256,2,1024]{2,1,0:T(2,128)}), f32[256,2,1024]{2,1,0:T(2,128)}, u32[]{:S(2)}, u32[]{:S(2)}) %all-to-all-start.2) | async-done | bytes 2097184 | tf_op jit(solution)/shard_map/all_to_all | solution.py:127
  293.6 8.6 %all-to-all-start.3 = ((f32[256,2,1024]{2,1,0:T(2,128)}), f32[256,2,1024]{2,1,0:T(2,128)}, u32[]{:S(2)}, u32[]{:S(2)}) async-start(f32[256,2,1024]{2,1,0:T(2,128)} %copy.61), calls=%async_computation.3 | async-start | bytes 4194304 | tf_op jit(solution)/shard_map/all_to_all | solution.py:128
  306.2 5.3 rev.15
  313.4 8.9 %rev.17 = f32[2,128,1024]{2,1,0:T(8,128)} reverse(f32[2,128,1024]{2,1,0:T(8,128)} %get-tuple-element.20), dimensions={0,1} | reverse | bytes 2097152 | tf_op jit(solution)/shard_map/rev | solution.py:46
  403.5 6.5 %multiply_add_fusion.2 = (f32[2,256,1024]{2,1,0:T(8,128)S(1)}, f32[2,256,1024]{2,1,0:T(8,128)S(1)}, f32[2,256,1024]{2,1,0:T(8,128)}, f32[2,256,1024]{2,1,0:T(8,128)}) fusion(f32[2,256,1024]{2,1,0:T(8,128)S(1)} %subtract_bitcast_fusion.2, f32[2,128,1024]{2,1,0:T(8,128)} %get-tuple-element.31, f32[2,128,1024]{2,1,0:T(8,128)S(1)} %copy-done.11, ...), kind=kOutput, calls=%fused_computation.14 | convolution fusion | flops 1617887232 | bytes 23069696 | tf_op jit(solution)/shard_map/rj,sjc->src/dot_general | solution.py:35
  423.7 6.0 add_bitcast_fusion.1
  434.0 14.4 %all-to-all-start.4 = ((f32[2,256,1024]{2,0,1:T(2,128)}), f32[2,256,1024]{2,0,1:T(2,128)}, u32[]{:S(2)}, u32[]{:S(2)}) async-start(f32[2,256,1024]{2,0,1:T(2,128)} %copy.67), calls=%async_computation.4 | async-start | bytes 4194304 | tf_op jit(solution)/shard_map/all_to_all | solution.py:180
  450.8 49.6 %all-to-all-done.4 = f32[2,256,1024]{2,0,1:T(2,128)} async-done(((f32[2,256,1024]{2,0,1:T(2,128)}), f32[2,256,1024]{2,0,1:T(2,128)}, u32[]{:S(2)}, u32[]{:S(2)}) %all-to-all-start.4) | async-done | bytes 2097184 | tf_op jit(solution)/shard_map/all_to_all | solution.py:180
  500.4 8.5 %all-to-all-start.5 = ((f32[2,256,1024]{2,0,1:T(2,128)}), f32[2,256,1024]{2,0,1:T(2,128)S(1)}, u32[]{:S(2)}, u32[]{:S(2)}) async-start(f32[2,256,1024]{2,0,1:T(2,128)} %copy.69), calls=%async_computation.5 | async-start | bytes 4194304 | tf_op jit(solution)/shard_map/all_to_all | solution.py:181
  519.5 41.6 %all-to-all-done.5 = f32[2,256,1024]{2,0,1:T(2,128)S(1)} async-done(((f32[2,256,1024]{2,0,1:T(2,128)}), f32[2,256,1024]{2,0,1:T(2,128)S(1)}, u32[]{:S(2)}, u32[]{:S(2)}) %all-to-all-start.5) | async-done | bytes 2097184 | tf_op jit(solution)/shard_map/all_to_all | solution.py:181
  571.7 8.2 %all-to-all-start.6 = ((bf16[128,2,1,1024]{3,1,2,0:T(2,128)(2,1)}), bf16[128,2,1,1024]{3,1,2,0:T(2,128)(2,1)S(1)}, u32[]{:S(2)}, u32[]{:S(2)}) async-start(bf16[128,2,1,1024]{3,1,2,0:T(2,128)(2,1)} %copy.71), calls=%async_computation.6 | async-start | bytes 1048576 | tf_op jit(solution)/shard_map/all_to_all | solution.py:189
  582.7 17.1 %all-to-all-done.6 = bf16[128,2,1,1024]{3,1,2,0:T(2,128)(2,1)S(1)} async-done(((bf16[128,2,1,1024]{3,1,2,0:T(2,128)(2,1)}), bf16[128,2,1,1024]{3,1,2,0:T(2,128)(2,1)S(1)}, u32[]{:S(2)}, u32[]{:S(2)}) %all-to-all-start.6) | async-done | bytes 524320 | tf_op jit(solution)/shard_map/all_to_all | solution.py:189
  605.5 6.4 %all-to-all-done.7 = bf16[1,2,128,1024]{3,2,0,1:T(8,128)(2,1)S(1)} async-done(((bf16[1,2,128,1024]{3,2,0,1:T(8,128)(2,1)}), bf16[1,2,128,1024]{3,2,0,1:T(8,128)(2,1)S(1)}, u32[]{:S(2)}, u32[]{:S(2)}) %all-to-all-start.7) | async-done | bytes 524320 | tf_op jit(solution)/shard_map/all_to_all | solution.py:188
  (117 shorter events, 195.8 us)
Async XLA Ops:
  2.5 21.7 %copy-start.14 = (bf16[128,2048]{1,0:T(8,128)(2,1)S(1)}, bf16[128,2048]{1,0:T(8,128)(2,1)}, u32[]{:S(2)}) copy-start(bf16[128,2048]{1,0:T(8,128)(2,1)} %param.3) | copy-start | bytes 1572868
  7.8 36.4 %all-to-all-start = ((bf16[128,2,1024]{2,1,0:T(2,128)(2,1)}), bf16[128,2,1024]{2,1,0:T(2,128)(2,1)S(1)}, u32[]{:S(2)}, u32[]{:S(2)}) async-start(bf16[128,2,1024]{2,1,0:T(2,128)(2,1)} %reshape.357), calls=%async_computation | async-start | bytes 1048576 | tf_op jit(solution)/shard_map/all_to_all | solution.py:79
  44.2 26.8 %all-to-all-start.8 = ((bf16[128,2,1024]{2,1,0:T(2,128)(2,1)}), bf16[128,2,1024]{2,1,0:T(2,128)(2,1)S(1)}, u32[]{:S(2)}, u32[]{:S(2)}) async-start(bf16[128,2,1024]{2,1,0:T(2,128)(2,1)} %reshape.361), calls=%async_computation.8 | async-start | bytes 1048576 | tf_op jit(solution)/shard_map/all_to_all | solution.py:66
  71.0 17.5 %all-to-all-start.1 = ((bf16[2,2,65536]{2,1,0:T(2,128)(2,1)}), bf16[2,2,65536]{2,1,0:T(2,128)(2,1)S(1)}, u32[]{:S(2)}, u32[]{:S(2)}) async-start(bf16[2,2,65536]{2,1,0:T(2,128)(2,1)} %reshape.359), calls=%async_computation.1 | async-start | bytes 1048576 | tf_op jit(solution)/shard_map/all_to_all | solution.py:78
  88.5 12.5 %all-to-all-start.9 = ((bf16[2,2,65536]{2,1,0:T(2,128)(2,1)}), bf16[2,2,65536]{2,1,0:T(2,128)(2,1)}, u32[]{:S(2)}, u32[]{:S(2)}) async-start(bf16[2,2,65536]{2,1,0:T(2,128)(2,1)} %reshape.363), calls=%async_computation.9 | async-start | bytes 1048576 | tf_op jit(solution)/shard_map/all_to_all | solution.py:65
  111.2 61.1 %all-to-all-start.11 = ((f32[256,2,1024]{2,1,0:T(2,128)}), f32[256,2,1024]{2,1,0:T(2,128)S(1)}, u32[]{:S(2)}, u32[]{:S(2)}) async-start(f32[256,2,1024]{2,1,0:T(2,128)} %copy.80), calls=%async_computation.11 | async-start | bytes 4194304 | tf_op jit(solution)/shard_map/all_to_all | solution.py:126
  172.3 60.6 %all-to-all-start.10 = ((f32[256,2,1024]{2,1,0:T(2,128)}), f32[256,2,1024]{2,1,0:T(2,128)}, u32[]{:S(2)}, u32[]{:S(2)}) async-start(f32[256,2,1024]{2,1,0:T(2,128)} %copy.78), calls=%async_computation.10 | async-start | bytes 4194304 | tf_op jit(solution)/shard_map/all_to_all | solution.py:125
  233.0 60.6 %all-to-all-start.2 = ((f32[256,2,1024]{2,1,0:T(2,128)}), f32[256,2,1024]{2,1,0:T(2,128)}, u32[]{:S(2)}, u32[]{:S(2)}) async-start(f32[256,2,1024]{2,1,0:T(2,128)} %copy.59), calls=%async_computation.2 | async-start | bytes 4194304 | tf_op jit(solution)/shard_map/all_to_all | solution.py:127
  293.6 94.6 %all-to-all-start.3 = ((f32[256,2,1024]{2,1,0:T(2,128)}), f32[256,2,1024]{2,1,0:T(2,128)}, u32[]{:S(2)}, u32[]{:S(2)}) async-start(f32[256,2,1024]{2,1,0:T(2,128)} %copy.61), calls=%async_computation.3 | async-start | bytes 4194304 | tf_op jit(solution)/shard_map/all_to_all | solution.py:128
  366.9 4.7 copy-start.1
  379.0 4.7 copy-start
  395.6 4.7 copy-start.2
  395.6 4.7 copy-start.7
  400.3 3.2 copy-start.3
  400.3 3.2 copy-start.5
  400.3 3.2 copy-start.10
  400.3 3.2 copy-start.11
  403.5 6.5 %copy-start.6 = (f32[2,256,1024]{2,1,0:T(8,128)}, f32[2,256,1024]{2,1,0:T(8,128)S(1)}, u32[]{:S(2)}) copy-start(f32[2,256,1024]{2,1,0:T(8,128)S(1)} %subtract_bitcast_fusion.2) | copy-start | bytes 6291460
  434.0 66.4 %all-to-all-start.4 = ((f32[2,256,1024]{2,0,1:T(2,128)}), f32[2,256,1024]{2,0,1:T(2,128)}, u32[]{:S(2)}, u32[]{:S(2)}) async-start(f32[2,256,1024]{2,0,1:T(2,128)} %copy.67), calls=%async_computation.4 | async-start | bytes 4194304 | tf_op jit(solution)/shard_map/all_to_all | solution.py:180
  500.4 60.7 %all-to-all-start.5 = ((f32[2,256,1024]{2,0,1:T(2,128)}), f32[2,256,1024]{2,0,1:T(2,128)S(1)}, u32[]{:S(2)}, u32[]{:S(2)}) async-start(f32[2,256,1024]{2,0,1:T(2,128)} %copy.69), calls=%async_computation.5 | async-start | bytes 4194304 | tf_op jit(solution)/shard_map/all_to_all | solution.py:181
  566.9 13.8 %copy-start.4 = (f32[2,256,1024]{2,1,0:T(8,128)S(1)}, f32[2,256,1024]{2,1,0:T(8,128)}, u32[]{:S(2)}) copy-start(f32[2,256,1024]{2,1,0:T(8,128)} %add_bitcast_fusion) | copy-start | bytes 6291460
  571.7 28.2 %all-to-all-start.6 = ((bf16[128,2,1,1024]{3,1,2,0:T(2,128)(2,1)}), bf16[128,2,1,1024]{3,1,2,0:T(2,128)(2,1)S(1)}, u32[]{:S(2)}, u32[]{:S(2)}) async-start(bf16[128,2,1,1024]{3,1,2,0:T(2,128)(2,1)} %copy.71), calls=%async_computation.6 | async-start | bytes 1048576 | tf_op jit(solution)/shard_map/all_to_all | solution.py:189
  582.7 21.5 %copy-start.9 = (f32[2,256,1024]{2,1,0:T(8,128)S(1)}, f32[2,256,1024]{2,1,0:T(8,128)}, u32[]{:S(2)}) copy-start(f32[2,256,1024]{2,1,0:T(8,128)} %get-tuple-element.16) | copy-start | bytes 6291460
  600.8 11.2 %all-to-all-start.7 = ((bf16[1,2,128,1024]{3,2,0,1:T(8,128)(2,1)}), bf16[1,2,128,1024]{3,2,0,1:T(8,128)(2,1)S(1)}, u32[]{:S(2)}, u32[]{:S(2)}) async-start(bf16[1,2,128,1024]{3,2,0,1:T(8,128)(2,1)} %copy.72), calls=%async_computation.7 | async-start | bytes 1048576 | tf_op jit(solution)/shard_map/all_to_all | solution.py:188
  (3 other events, 6.5 us)
where the time goes:
time: 625 us; the launch traced here: 613 us
  waiting for transfers between devices  280 us (45%)
  local copies, waits for them, and re-layouts  117 us (19%)
  starting transfers between devices  101 us (16%)
  matrix products  72.1 us (12%)
  other arithmetic  42.3 us (7%)
    dot_general x14, matrix products, einsum_exact(): jnp.einsum(form, left, right, precision=exact_mode, preferred_element_typ...  62 us
    all_to_all x1, waiting for transfers between devices, local(): lax.all_to_all(back_real, 'seq', split_axis=1, concat_axis=0, tiled=True)  49.6 us
    all_to_all x1, waiting for transfers between devices, local(): lax.all_to_all(input_imag, 'seq', split_axis=0, concat_axis=1, tiled=True)  47.7 us
    all_to_all x1, waiting for transfers between devices, local(): lax.all_to_all(cotan_real, 'seq', split_axis=0, concat_axis=1, tiled=True)  47.4 us
    all_to_all x1, waiting for transfers between devices, local(): lax.all_to_all(input_real, 'seq', split_axis=0, concat_axis=1, tiled=True)  47.4 us
    all_to_all x1, waiting for transfers between devices, local(): lax.all_to_all(back_imag, 'seq', split_axis=1, concat_axis=0, tiled=True)  41.6 us
    unnamed x4, other arithmetic  30.1 us
    all_to_all x1, waiting for transfers between devices, local(): lax.all_to_all(spatial, 'seq', split_axis=0, concat_axis=2, tiled=True)  17.1 us
  transfers between devices with their start and end apart: 12, of which 10 were waited for; matrix products, arithmetic and copies ran while one was open for 23% of the time, Pallas kernels for 0%

commit v1 on v0

v1 whole, which is shorter than its diff:
```python
import functools

import jax
import jax.numpy as jnp
import ml_dtypes
import numpy as np
from jax import lax
from jax.experimental import pallas as pl
from jax.experimental.pallas import tpu as pltpu
from jax.sharding import PartitionSpec as P

MESH = pl.DeviceIdType.MESH
OWN = 8
LANES = 128
F32 = jnp.float32
BF16 = jnp.bfloat16


def split(table):
    high = table.astype(ml_dtypes.bfloat16)
    low = (table - high.astype(np.float64)).astype(ml_dtypes.bfloat16)
    return high, low


def angles(left, right, modulus):
    return 2.0 * np.pi * (np.outer(left, right) % modulus) / modulus


@functools.cache
def tables(shards, width):
    classes, offsets = 2 * shards, 2 * width
    points = classes * offsets
    c = np.arange(shards)
    p = np.arange(shards)
    j = np.arange(offsets)
    r = np.arange(width)
    turn = angles(c, p, classes)
    first = np.concatenate([np.cos(turn), -np.sin(turn)])
    first[shards] = np.cos(np.pi * p)
    last = np.concatenate([2.0 * np.cos(turn.T), -2.0 * np.sin(turn.T)], axis=1)
    last[:, 0] = 1.0
    last[:, shards] = np.cos(np.pi * p)
    twist = angles(np.arange(shards + 1), j, points)
    twist_cos, twist_sin = np.cos(twist), -np.sin(twist)
    low, up = angles(j, r, offsets), angles(j, r + 1, offsets)
    inner = np.block(
        [
            [np.cos(low), -np.sin(low), np.cos(up), -np.sin(up)],
            [np.sin(low), np.cos(low), -np.sin(up), -np.cos(up)],
        ]
    )
    edge = np.stack([twist_cos[shards], twist_sin[shards]] + [np.zeros(offsets)] * 6)
    first_high, first_low = split(first)
    last_high, last_low = split(last)
    inner_high, inner_low = split(inner)
    return (
        np.concatenate([first_high, first_low], axis=1),
        np.concatenate([last_high, last_low], axis=0),
        np.stack([inner_high, inner_low]),
        np.stack([inner_high.T, inner_low.T]),
        np.stack([twist_cos[:shards], twist_sin[:shards]]).astype(np.float32),
        edge.astype(np.float32),
    )


def halves(value):
    high = value.astype(BF16)
    return high, (value - high.astype(F32)).astype(BF16)


def dot(left, right):
    return jnp.dot(left, right, preferred_element_type=F32)


def dot3(left_high, left_low, right_ref):
    return (
        dot(left_high, right_ref[0]) + dot(left_high, right_ref[1]) + dot(left_low, right_ref[0])
    )


def kernel(
    shards,
    x_hbm,
    ct_hbm,
    f_hbm,
    first_hbm,
    last_hbm,
    inner_hbm,
    outer_hbm,
    twist_hbm,
    edge_hbm,
    gi_hbm,
    gf_hbm,
    x_v,
    f_v,
    first,
    last,
    inner,
    outer,
    twist,
    edge,
    x_out,
    x_got,
    f_out,
    f_got,
    g_out,
    g_got,
    y_out,
    y_got,
    wide,
    z_high,
    z_low,
    spec,
    f_wide,
    g_wide,
    w_high,
    w_low,
    back,
    y_wide,
    gi_v,
    gf_v,
    load_sem,
    send_sem,
    recv_sem,
    store_sem,
):
    width = LANES
    all_devices = 2 * shards
    points = 4 * shards * width
    both = 2 * OWN
    s, h = lax.axis_index("seq"), lax.axis_index("chan")
    me = 2 * s + h
    own = h * shards + s

    loads = [
        pltpu.make_async_copy(source, target, load_sem.at[at])
        for at, (source, target) in enumerate(
            (
                (x_hbm, x_v.at[0]),
                (ct_hbm, x_v.at[1]),
                (f_hbm, f_v),
                (first_hbm, first),
                (last_hbm, last),
                (inner_hbm, inner),
                (outer_hbm, outer),
                (twist_hbm, twist),
                (edge_hbm, edge),
            )
        )
    ]
    for load in loads:
        load.start()

    barrier = pltpu.get_barrier_semaphore()

    def greet(k, carry):
        t = (me + k) % all_devices
        pl.semaphore_signal(barrier, inc=1, device_id=(t // 2, t % 2), device_id_type=MESH)
        return carry

    lax.fori_loop(1, all_devices, greet, 0)

    def remote(phase, source, target, device):
        return pltpu.make_async_remote_copy(
            src_ref=source,
            dst_ref=target,
            send_sem=send_sem.at[phase],
            recv_sem=recv_sem.at[phase],
            device_id=device,
            device_id_type=MESH,
        )

    def to_all(phase, out, got):
        def send(k, carry):
            t = (me + k) % all_devices
            remote(phase, out.at[t % 2 * shards + t // 2], got.at[own], (t // 2, t % 2)).start()
            return carry

        lax.fori_loop(1, all_devices, send, 0)

    def to_row(phase, out, got):
        def send(k, carry):
            t = (s + k) % shards
            remote(phase, out.at[t], got.at[s], (t, h)).start()
            return carry

        lax.fori_loop(1, shards, send, 0)

    def whole(phase, out, got, count):
        rest = pl.ds(0, count - 1)
        return remote(phase, out.at[rest], got.at[rest], ((s + 1) % shards, h))

    loads[0].wait()
    loads[1].wait()

    def turn_x(t, carry):
        at = pl.ds(pl.multiple_of(t * LANES, LANES), LANES)
        parts = [x_v[a, :, at].astype(F32).T.reshape(LANES // OWN, OWN, width) for a in range(2)]
        x_out[pl.ds(t * (LANES // OWN), LANES // OWN)] = jnp.concatenate(parts, axis=1).astype(BF16)
        return carry

    lax.fori_loop(0, all_devices * OWN // LANES, turn_x, 0)
    x_got[own] = x_out[own]
    pl.semaphore_wait(barrier, all_devices - 1)
    to_all(0, x_out, x_got)

    loads[2].wait()

    def turn_f(t, carry):
        at = pl.ds(pl.multiple_of(t * LANES, LANES), LANES)
        for g in range(2):
            parts = [
                f_v[part, g, :, at].astype(F32).T.reshape(LANES // OWN, OWN, width)
                for part in range(2)
            ]
            f_out[pl.ds(t * (LANES // OWN), LANES // OWN), g] = jnp.concatenate(
                parts, axis=1
            ).astype(BF16)
        return carry

    lax.fori_loop(0, shards * OWN // LANES, turn_f, 0)
    f_got[s] = f_out[s]
    to_row(1, f_out, f_got)
    for load in loads[3:]:
        load.wait()

    whole(0, x_out, x_got, all_devices).wait_recv()

    def widen_x(t, carry):
        rows = pl.ds(pl.multiple_of(t * 16 * both, 16 * both), 16 * both)
        wide[rows] = x_got[pl.ds(t * 16, 16)].astype(F32).reshape(16 * both, width)
        return carry

    lax.fori_loop(0, all_devices // 16, widen_x, 0)

    def forward_first(q, carry):
        x = jnp.concatenate(
            [wide[pl.ds(a * shards * both + q, shards, stride=both), :] for a in range(2)], axis=1
        ).astype(BF16)
        y = dot(first[...], jnp.concatenate([x, x], axis=0))
        real, imag = y[:shards], y[shards:]
        alone = imag[0:1]
        zero_row = lax.broadcasted_iota(jnp.int32, imag.shape, 0) == 0
        imag = jnp.where(zero_row, 0.0, imag)
        z = jnp.concatenate(
            [real * twist[0] - imag * twist[1], real * twist[1] + imag * twist[0]], axis=1
        )
        rows = pl.ds(pl.multiple_of(q * shards, shards), shards)
        high, low = halves(z)
        z_high[rows] = high
        z_low[rows] = low
        spec[pl.ds(both * shards + q, 1), :] = jnp.concatenate(
            [alone * edge[0:1], alone * edge[1:2]], axis=1
        )
        return carry

    lax.fori_loop(0, both, forward_first, 0)
    tail = pl.ds(both * shards, both)
    high, low = halves(spec[tail])
    z_high[tail] = high
    z_low[tail] = low

    rows_forward = z_high.shape[0]
    step_forward = rows_forward // 3 if rows_forward % 48 == 0 else rows_forward

    def forward_second(t, carry):
        rows = pl.ds(pl.multiple_of(t * step_forward, 16), step_forward)
        spec[rows] = dot3(z_high[rows], z_low[rows], inner)
        return carry

    lax.fori_loop(0, rows_forward // step_forward, forward_second, 0)

    for q in range(both):
        zero, extra = pl.ds(q * shards, 1), pl.ds(both * shards + q, 1)
        kept = spec[zero, 2 * width : 3 * width]
        spec[zero, 2 * width :] = spec[extra, : 2 * width]
        spec[extra, 2 * width : 3 * width] = kept

    corner = (lax.broadcasted_iota(jnp.int32, (shards, width), 0) == 0) & (
        lax.broadcasted_iota(jnp.int32, (shards, width), 1) == 0
    )

    def spectrum(q, g):
        rows = pl.ds(pl.multiple_of(q * shards, shards), shards)
        at = 2 * width * g
        return spec[rows, at : at + width], spec[rows, at + width : at + 2 * width]

    def top(q):
        return spec[pl.ds(both * shards + q, 1), 3 * width - 1 : 3 * width]

    for ch in range(OWN):
        for g in range(2):
            (ur, ui), (vr, vi) = spectrum(ch, g), spectrum(OWN + ch, g)
            real = (ur * vr + ui * vi) * (2.0 / points)
            imag = (ur * vi - ui * vr) * (2.0 / points)
            if g == 0:
                real = jnp.where(corner, 0.5 * real, real)
                imag = jnp.where(corner, top(ch) * top(OWN + ch) * (1.0 / points), imag)
            g_wide[g, pl.ds(ch, shards, stride=both), :] = real
            g_wide[g, pl.ds(OWN + ch, shards, stride=both), :] = imag

    def narrow_g(t, carry):
        rows = pl.ds(pl.multiple_of(t * 16 * both, 16 * both), 16 * both)
        for g in range(2):
            g_out[pl.ds(t * 16, 16), g] = g_wide[g, rows].reshape(16, both, width).astype(BF16)
        return carry

    lax.fori_loop(0, shards // 16, narrow_g, 0)
    g_got[s] = g_out[s]
    to_row(2, g_out, g_got)

    whole(1, f_out, f_got, shards).wait_recv()

    def widen_f(t, carry):
        rows = pl.ds(pl.multiple_of(t * 16 * both, 16 * both), 16 * both)
        for g in range(2):
            f_wide[g, rows] = f_got[pl.ds(t * 16, 16), g].astype(F32).reshape(16 * both, width)
        return carry

    lax.fori_loop(0, shards // 16, widen_f, 0)

    row_at = lax.broadcasted_iota(jnp.int32, (shards, width), 0)
    lane_at = lax.broadcasted_iota(jnp.int32, (shards, width), 1)
    lane_one = lax.broadcasted_iota(jnp.int32, (1, width), 1)
    extra_rows = w_high.shape[0] - OWN * shards
    back[pl.ds(OWN * shards, extra_rows)] = jnp.zeros((extra_rows, 4 * width), F32)
    for ch in range(OWN):
        fields = []
        for g in range(2):
            vr, vi = spectrum(OWN + ch, g)
            fr = f_wide[g, pl.ds(ch, shards, stride=both), :]
            fi = f_wide[g, pl.ds(OWN + ch, shards, stride=both), :]
            if g == 0:
                above = top(OWN + ch) * fi[0:1, 0:1]
                fi = jnp.where(corner, 0.0, fi)
            fields.append((fr * vr + fi * vi, fr * vi - fi * vr))
        (ar, ai), (br, bi) = fields
        back[pl.ds(OWN * shards + ch, 1), : 2 * width] = 2.0 * jnp.concatenate(
            [br[0:1], bi[0:1]], axis=1
        )
        twice = (row_at == 0) & (lane_at > 0)
        ar = jnp.where(twice, 2.0 * ar, ar)
        ai = jnp.where(twice, 2.0 * ai, jnp.where(corner, 0.0, ai))
        br = jnp.where(row_at == 0, jnp.where(lane_one == width - 1, above, 0.0), br)
        bi = jnp.where(row_at == 0, 0.0, bi)
        high, low = halves(jnp.concatenate([ar, ai, br, bi], axis=1))
        rows = pl.ds(ch * shards, shards)
        w_high[rows] = high
        w_low[rows] = low
    tail_back = pl.ds(OWN * shards, extra_rows)
    high, low = halves(back[tail_back])
    w_high[tail_back] = high
    w_low[tail_back] = low

    rows_back = w_high.shape[0]
    step_back = rows_back // 3 if rows_back % 48 == 0 else rows_back

    def inverse_first(t, carry):
        rows = pl.ds(pl.multiple_of(t * step_back, 16), step_back)
        back[rows] = dot3(w_high[rows], w_low[rows], outer)
        return carry

    lax.fori_loop(0, rows_back // step_back, inverse_first, 0)

    for ch in range(OWN):
        rows = pl.ds(ch * shards, shards)
        hr, hi = back[rows, : 2 * width], back[rows, 2 * width :]
        extra = pl.ds(OWN * shards + ch, 1)
        er, ei = back[extra, : 2 * width], back[extra, 2 * width :]
        kr = hr * twist[0] + hi * twist[1]
        ki = hi * twist[0] - hr * twist[1]
        zero_row = lax.broadcasted_iota(jnp.int32, ki.shape, 0) == 0
        ki = jnp.where(zero_row, er * edge[0:1] + ei * edge[1:2], ki)
        high, low = halves(jnp.concatenate([kr, ki], axis=0))
        main = dot(last[...], high)
        y = main[:shards] + main[shards:] + dot(last[pl.ds(0, shards)], low)
        y = y * (1.0 / points)
        for a in range(2):
            y_wide[a, pl.ds(ch, shards, stride=OWN), :] = y[:, a * width : (a + 1) * width]

    def narrow_y(t, carry):
        rows = pl.ds(pl.multiple_of(t * 16 * OWN, 16 * OWN), 16 * OWN)
        for a in range(2):
            y_out[pl.ds(a * shards + t * 16, 16)] = (
                y_wide[a, rows].reshape(16, OWN, width).astype(BF16)
            )
        return carry

    lax.fori_loop(0, shards // 16, narrow_y, 0)
    y_got[own] = y_out[own]
    to_all(3, y_out, y_got)

    whole(2, g_out, g_got, shards).wait_recv()

    def turn_g(t, carry):
        at = pl.ds(pl.multiple_of(t * LANES, LANES), LANES)
        for g in range(2):
            block = g_got[pl.ds(t * (LANES // OWN), LANES // OWN), g].astype(F32)
            for part in range(2):
                rows = block[:, part * OWN : (part + 1) * OWN].reshape(LANES, width)
                gf_v[part, g, :, at] = rows.T.astype(BF16)
        return carry

    lax.fori_loop(0, shards * OWN // LANES, turn_g, 0)
    store_gf = pltpu.make_async_copy(gf_v, gf_hbm, store_sem.at[0])
    store_gf.start()

    whole(3, y_out, y_got, all_devices).wait_recv()

    def turn_y(t, carry):
        at = pl.ds(pl.multiple_of(t * LANES, LANES), LANES)
        rows = y_got[pl.ds(t * (LANES // OWN), LANES // OWN)].astype(F32).reshape(LANES, width)
        gi_v[:, at] = rows.T.astype(BF16)
        return carry

    lax.fori_loop(0, all_devices * OWN // LANES, turn_y, 0)
    store_gi = pltpu.make_async_copy(gi_v, gi_hbm, store_sem.at[1])
    store_gi.start()

    whole(0, x_out, x_got, all_devices).wait_send()
    whole(1, f_out, f_got, shards).wait_send()
    whole(2, g_out, g_got, shards).wait_send()
    whole(3, y_out, y_got, all_devices).wait_send()
    store_gf.wait()
    store_gi.wait()


def local(inputs, cotangent, filter_spec):
    width, channels = inputs.shape
    shards = lax.axis_size("seq")
    group = channels // 2
    both = 2 * OWN
    constants = [jnp.asarray(table) for table in tables(shards, width)]
    extra = 32
    scratch = [
        ((2, width, channels), BF16),
        ((2, 2, width, group), BF16),
        *[(tuple(table.shape), table.dtype) for table in constants],
        ((2 * shards, both, width), BF16),
        ((2 * shards, both, width), BF16),
        ((shards, 2, both, width), BF16),
        ((shards, 2, both, width), BF16),
        ((shards, 2, both, width), BF16),
        ((shards, 2, both, width), BF16),
        ((2 * shards, OWN, width), BF16),
        ((2 * shards, OWN, width), BF16),
        ((2 * shards * both, width), F32),
        ((both * shards + both, 4 * width), BF16),
        ((both * shards + both, 4 * width), BF16),
        ((both * shards + both, 4 * width), F32),
        ((2, shards * both, width), F32),
        ((2, shards * both, width), F32),
        ((OWN * shards + extra, 4 * width), BF16),
        ((OWN * shards + extra, 4 * width), BF16),
        ((OWN * shards + extra, 4 * width), F32),
        ((2, shards * OWN, width), F32),
        ((width, channels), BF16),
        ((2, 2, width, group), BF16),
    ]
    return pl.pallas_call(
        functools.partial(kernel, shards),
        out_shape=(
            jax.ShapeDtypeStruct((width, channels), BF16),
            jax.ShapeDtypeStruct((2, 2, width, group), BF16),
        ),
        in_specs=[pl.BlockSpec(memory_space=pl.ANY)] * 9,
        out_specs=[pl.BlockSpec(memory_space=pl.ANY)] * 2,
        scratch_shapes=[pltpu.VMEM(shape, dtype) for shape, dtype in scratch]
        + [
            pltpu.SemaphoreType.DMA((9,)),
            pltpu.SemaphoreType.DMA((4,)),
            pltpu.SemaphoreType.DMA((4,)),
            pltpu.SemaphoreType.DMA((2,)),
        ],
        compiler_params=pltpu.CompilerParams(
            collective_id=0, has_side_effects=True, vmem_limit_bytes=48 << 20
        ),
        name="hyena_backward",
    )(inputs, cotangent, filter_spec, *constants)


def solution(mesh):
    return jax.shard_map(
        local,
        mesh=mesh,
        in_specs=(P(("seq", "chan"), None), P(("seq", "chan"), None), P(None, "seq", None, "chan")),
        out_specs=(P(("seq", "chan"), None), P(None, "seq", None, "chan")),
        check_vma=False,
    )
```

time: 625 us -> 110 us (0.18); the launches traced: 613 us -> 110 us
  waiting for transfers between devices: 280 us -> 0 us
  local copies, waits for them, and re-layouts: 117 us -> 9.75 us
  starting transfers between devices: 101 us -> 0 us
  Pallas kernels: 0 us -> 99.4 us
  matrix products: 72.1 us -> 0 us
  other arithmetic: 42.3 us -> 0 us
    all_to_all x12 -> x0, waiting for transfers between devices: 280 us -> none  [the longest x1 49.6 us: local(): lax.all_to_all(back_real, 'seq', split_axis=1, concat_axis=0, tiled=True)]
    all_to_all x12 -> x0, starting transfers between devices: 101 us -> none  [the longest x1 16.4 us: local(): lax.all_to_all(cotangent.reshape(1, 1, tok_count, full_width), 'seq', spl...]
    pallas_call x0 -> x1, Pallas kernels: none -> 99.4 us  [local(): pl.pallas_call(functools.partial(kernel, shards), out_shape=(jax.ShapeDty...]
    dot_general x18 -> x0, matrix products: 72.1 us -> none  [the longest x14 62 us: einsum_exact(): jnp.einsum(form, left, right, precision=exact_mode, preferred_element_typ...]
    all_to_all x16 -> x0, local copies, waits for them, and re-layouts: 40.6 us -> none  [the longest x2 7.37 us: local(): lax.all_to_all(cotan_imag, 'seq', split_axis=0, concat_axis=1, tiled=True)]
    unnamed x4 -> x0, other arithmetic: 30.1 us -> none
    rev x4 -> x0, local copies, waits for them, and re-layouts: 23.7 us -> none  [the longest x2 14.2 us: mirror(): generic = values[::-1, ::-1]]
    slice x7 -> x0, local copies, waits for them, and re-layouts: 15.5 us -> none  [the longest x6 14.6 us: mirror(): special = jnp.stack([jnp.roll(values[0, ::-1], 1, axis=0), values[1, ::-1]])]
  transfers between devices with their start and end apart: 12 -> 0, of which waited for: 10 -> 0; matrix products, arithmetic and copies ran while one was open for 23% -> 0% of each run, Pallas kernels for 0% -> 0%
where the time goes in v1:
time: 110 us
  Pallas kernels  99.4 us (90%)
  local copies, waits for them, and re-layouts  9.75 us (9%)
    pallas_call x1, Pallas kernels, local(): pl.pallas_call(functools.partial(kernel, shards), out_shape=(jax.ShapeDty...  99.4 us
    unnamed x18, local copies, waits for them, and re-layouts  9.75 us

profile of v1, /device:TPU:1, one launch (start us, length us, event | category | flops | bytes accessed | tf_op | source)
XLA Modules:
  0.0 109.8 jit_solution(7409540985931742211)
XLA Ops:
  0.6 0.0 copy-start.7
  0.6 0.7 copy-done.7
  1.3 0.0 copy-start
  1.3 1.2 %copy-done = bf16[2,2,128,1024]{3,2,1,0:T(8,128)(2,1)S(1)} copy-done((bf16[2,2,128,1024]{3,2,1,0:T(8,128)(2,1)S(1)}, bf16[2,2,128,1024]{3,2,1,0:T(8,128)(2,1)}, u32[]{:S(2)}) %copy-start) | copy-done | bytes 1048600
  2.6 0.0 copy-start.1
  2.6 1.2 %copy-done.1 = bf16[2,512,512]{2,1,0:T(8,128)(2,1)S(1)} copy-done((bf16[2,512,512]{2,1,0:T(8,128)(2,1)S(1)}, bf16[2,512,512]{2,1,0:T(8,128)(2,1)}, u32[]{:S(2)}) %copy-start.1) | copy-done | bytes 1048600
  3.8 0.0 copy-start.2
  3.8 1.0 copy-done.2
  4.8 0.0 copy-start.3
  4.8 1.0 copy-done.3
  5.9 0.0 copy-start.4
  5.9 0.9 copy-done.4
  6.8 0.0 copy-start.5
  6.8 0.9 copy-done.5
  7.7 0.0 copy-start.6
  7.7 0.9 copy-done.6
  8.6 99.4 %hyena_backward.1 = (bf16[128,2048]{1,0:T(8,128)(2,1)S(1)}, bf16[2,2,128,1024]{3,2,1,0:T(8,128)(2,1)S(1)}) custom-call(bf16[128,2048]{1,0:T(8,128)(2,1)S(1)} %copy-done.2, bf16[128,2048]{1,0:T(8,128)(2,1)S(1)} %copy-done.3, bf16[2,2,128,1024]{3,2,1,0:T(8,128)(2,1)S(1)} %copy-done, bf16[256,256]{1,0:T(8,128)(2,1)S(1)} %copy-done.6, ...), custom_call_target="tpu_custom_call" | custom-call | tf_op jit(solution)/shard_map/hyena_backward/pallas_call | solution.py:460
  108.0 0.8 copy.13
  108.8 1.0 copy.14
Async XLA Ops:
  0.6 0.7 copy-start.7
  1.3 1.2 %copy-start = (bf16[2,2,128,1024]{3,2,1,0:T(8,128)(2,1)S(1)}, bf16[2,2,128,1024]{3,2,1,0:T(8,128)(2,1)}, u32[]{:S(2)}) copy-start(bf16[2,2,128,1024]{3,2,1,0:T(8,128)(2,1)} %f_hbm.1) | copy-start | bytes 3145732
  2.6 1.2 %copy-start.1 = (bf16[2,512,512]{2,1,0:T(8,128)(2,1)S(1)}, bf16[2,512,512]{2,1,0:T(8,128)(2,1)}, u32[]{:S(2)}) copy-start(bf16[2,512,512]{2,1,0:T(8,128)(2,1)} %constant.14.clone.inner_hbm) | copy-start | bytes 3145732
  3.8 1.0 copy-start.2
  4.8 1.0 copy-start.3
  5.9 0.9 copy-start.4
  6.8 0.9 copy-start.5
  7.7 0.9 copy-start.6

commit v2 on v1

--- a/solution.py
+++ b/solution.py
@@ -12,6 +12,7 @@
 MESH = pl.DeviceIdType.MESH
 OWN = 8
 LANES = 128
+COLUMN = 16
 F32 = jnp.float32
 BF16 = jnp.bfloat16
 
@@ -122,15 +123,20 @@
     load_sem,
     send_sem,
     recv_sem,
+    y_sem,
     store_sem,
+    plane_sem,
 ):
     width = LANES
     all_devices = 2 * shards
     points = 4 * shards * width
     both = 2 * OWN
+    columns = shards // COLUMN
+    planes = 2 * columns
     s, h = lax.axis_index("seq"), lax.axis_index("chan")
-    me = 2 * s + h
     own = h * shards + s
+    spot, column = lax.rem(s, COLUMN), lax.div(s, COLUMN)
+    place = 2 * column + h
 
     loads = [
         pltpu.make_async_copy(source, target, load_sem.at[at])
@@ -153,60 +159,62 @@
 
     barrier = pltpu.get_barrier_semaphore()
 
-    def greet(k, carry):
-        t = (me + k) % all_devices
-        pl.semaphore_signal(barrier, inc=1, device_id=(t // 2, t % 2), device_id_type=MESH)
-        return carry
-
-    lax.fori_loop(1, all_devices, greet, 0)
-
-    def remote(phase, source, target, device):
+    def in_column(k):
+        return column * COLUMN + lax.rem(spot + k, COLUMN), h
+
+    def in_plane(k):
+        t = lax.rem(place + k, planes)
+        return lax.div(t, 2) * COLUMN + spot, lax.rem(t, 2)
+
+    def signal(semaphore, device):
+        pl.semaphore_signal(semaphore, inc=1, device_id=device, device_id_type=MESH)
+
+    for k in range(1, COLUMN):
+        signal(barrier, in_column(k))
+    for k in range(1, planes):
+        signal(barrier, in_plane(k))
+
+    def remote(phase, source, target, device, arrival=None):
         return pltpu.make_async_remote_copy(
             src_ref=source,
             dst_ref=target,
             send_sem=send_sem.at[phase],
-            recv_sem=recv_sem.at[phase],
+            recv_sem=recv_sem.at[phase] if arrival is None else arrival,
             device_id=device,
             device_id_type=MESH,
         )
 
-    def to_all(phase, out, got):
-        def send(k, carry):
-            t = (me + k) % all_devices
-            remote(phase, out.at[t % 2 * shards + t // 2], got.at[own], (t // 2, t % 2)).start()
+    def to_column(phase, out, got, k, first_spot, arrival=None):
+        t = lax.rem(place + k, planes)
+        peer_h, start = lax.rem(t, 2), lax.div(t, 2) * COLUMN
+        base = peer_h * shards + start
+        for j in range(first_spot, COLUMN):
+            at = lax.rem(spot + j, COLUMN)
+            remote(phase, out.at[base + at], got.at[own], (start + at, peer_h), arrival).start()
+
+    def to_row(phase, out, got, k, first_spot):
+        start = lax.rem(column + k, columns) * COLUMN
+        for j in range(first_spot, COLUMN):
+            at = start + lax.rem(spot + j, COLUMN)
+            remote(phase, out.at[at], got.at[s], (at, h)).start()
+
+    def rest(count, step):
+        def body(k, carry):
+            step(k)
             return carry
 
-        lax.fori_loop(1, all_devices, send, 0)
-
-    def to_row(phase, out, got):
-        def send(k, carry):
-            t = (s + k) % shards
-            remote(phase, out.at[t], got.at[s], (t, h)).start()
-            return carry
-
-        lax.fori_loop(1, shards, send, 0)
+        lax.fori_loop(1, count, body, 0)
 
     def whole(phase, out, got, count):
-        rest = pl.ds(0, count - 1)
-        return remote(phase, out.at[rest], got.at[rest], ((s + 1) % shards, h))
-
-    loads[0].wait()
-    loads[1].wait()
-
-    def turn_x(t, carry):
+        some = pl.ds(0, count - 1)
+        return remote(phase, out.at[some], got.at[some], in_plane(1))
+
+    def turn_x(t):
         at = pl.ds(pl.multiple_of(t * LANES, LANES), LANES)
         parts = [x_v[a, :, at].astype(F32).T.reshape(LANES // OWN, OWN, width) for a in range(2)]
         x_out[pl.ds(t * (LANES // OWN), LANES // OWN)] = jnp.concatenate(parts, axis=1).astype(BF16)
-        return carry
-
-    lax.fori_loop(0, all_devices * OWN // LANES, turn_x, 0)
-    x_got[own] = x_out[own]
-    pl.semaphore_wait(barrier, all_devices - 1)
-    to_all(0, x_out, x_got)
-
-    loads[2].wait()
-
-    def turn_f(t, carry):
+
+    def turn_f(t):
         at = pl.ds(pl.multiple_of(t * LANES, LANES), LANES)
         for g in range(2):
             parts = [
@@ -216,11 +224,24 @@
             f_out[pl.ds(t * (LANES // OWN), LANES // OWN), g] = jnp.concatenate(
                 parts, axis=1
             ).astype(BF16)
-        return carry
-
-    lax.fori_loop(0, shards * OWN // LANES, turn_f, 0)
+
+    loads[0].wait()
+    loads[1].wait()
+    turn_x(h * columns + column)
+    loads[2].wait()
+    turn_f(column)
+    rest(planes, lambda k: turn_x(lax.rem(h * columns + column + k, planes)))
+    pl.semaphore_wait(barrier, COLUMN - 1 + planes - 1)
+    for k in range(1, planes):
+        signal(plane_sem, in_plane(k))
+    to_column(0, x_out, x_got, 0, 1)
+    to_row(1, f_out, f_got, 0, 1)
+    rest(columns, lambda k: turn_f(lax.rem(column + k, columns)))
+    x_got[own] = x_out[own]
     f_got[s] = f_out[s]
-    to_row(1, f_out, f_got)
+    pl.semaphore_wait(plane_sem, planes - 1)
+    rest(planes, lambda k: to_column(0, x_out, x_got, k, 0))
+    rest(columns, lambda k: to_row(1, f_out, f_got, k, 0))
     for load in loads[3:]:
         load.wait()
 
@@ -307,7 +328,8 @@
 
     lax.fori_loop(0, shards // 16, narrow_g, 0)
     g_got[s] = g_out[s]
-    to_row(2, g_out, g_got)
+    rest(columns, lambda k: to_row(2, g_out, g_got, k, 0))
+    to_row(2, g_out, g_got, 0, 1)
 
     whole(1, f_out, f_got, shards).wait_recv()
 
@@ -388,7 +410,9 @@
 
     lax.fori_loop(0, shards // 16, narrow_y, 0)
     y_got[own] = y_out[own]
-    to_all(3, y_out, y_got)
+    mine = h * columns + column
+    rest(planes, lambda k: to_column(3, y_out, y_got, k, 0, y_sem.at[mine]))
+    to_column(3, y_out, y_got, 0, 1, y_sem.at[mine])
 
     whole(2, g_out, g_got, shards).wait_recv()
 
@@ -402,27 +426,30 @@
         return carry
 
     lax.fori_loop(0, shards * OWN // LANES, turn_g, 0)
+
     store_gf = pltpu.make_async_copy(gf_v, gf_hbm, store_sem.at[0])
     store_gf.start()
 
-    whole(3, y_out, y_got, all_devices).wait_recv()
-
-    def turn_y(t, carry):
+    def turn_y(k, missing):
+        t = lax.rem(place - k + planes, planes)
+        t = lax.rem(t, 2) * columns + lax.div(t, 2)
+        first_row = t * COLUMN
+        some = pl.ds(first_row, COLUMN - missing)
+        remote(3, y_out.at[some], y_got.at[some], in_plane(1), y_sem.at[t]).wait_recv()
         at = pl.ds(pl.multiple_of(t * LANES, LANES), LANES)
-        rows = y_got[pl.ds(t * (LANES // OWN), LANES // OWN)].astype(F32).reshape(LANES, width)
+        rows = y_got[pl.ds(first_row, COLUMN)].astype(F32).reshape(LANES, width)
         gi_v[:, at] = rows.T.astype(BF16)
-        return carry
-
-    lax.fori_loop(0, all_devices * OWN // LANES, turn_y, 0)
-    store_gi = pltpu.make_async_copy(gi_v, gi_hbm, store_sem.at[1])
-    store_gi.start()
+        pltpu.make_async_copy(gi_v.at[:, at], gi_hbm.at[:, at], store_sem.at[1]).start()
+
+    rest(planes, lambda k: turn_y(k, 0))
+    turn_y(0, 1)
 
     whole(0, x_out, x_got, all_devices).wait_send()
     whole(1, f_out, f_got, shards).wait_send()
     whole(2, g_out, g_got, shards).wait_send()
     whole(3, y_out, y_got, all_devices).wait_send()
     store_gf.wait()
-    store_gi.wait()
+    pltpu.make_async_copy(gi_v, gi_hbm, store_sem.at[1]).wait()
 
 
 def local(inputs, cotangent, filter_spec):
@@ -469,11 +496,13 @@
         + [
             pltpu.SemaphoreType.DMA((9,)),
             pltpu.SemaphoreType.DMA((4,)),
-            pltpu.SemaphoreType.DMA((4,)),
+            pltpu.SemaphoreType.DMA((3,)),
+            pltpu.SemaphoreType.DMA((2 * shards // COLUMN,)),
             pltpu.SemaphoreType.DMA((2,)),
+            pltpu.SemaphoreType.REGULAR,
         ],
         compiler_params=pltpu.CompilerParams(
-            collective_id=0, has_side_effects=True, vmem_limit_bytes=48 << 20
+            collective_id=0, has_side_effects=True, vmem_limit_bytes=60 << 20
         ),
         name="hyena_backward",
     )(inputs, cotangent, filter_spec, *constants)

time: 110 us -> 97.7 us (0.89)
  local copies, waits for them, and re-layouts: 9.75 us -> 2.94 us
  Pallas kernels: 99.4 us -> 94 us
    unnamed x18 -> x4, local copies, waits for them, and re-layouts: 9.75 us -> 2.94 us
    pallas_call x1, Pallas kernels: 99.4 us -> 94 us  [local(): pl.pallas_call(functools.partial(kernel, shards), out_shape=(jax.ShapeDty...]
where the time goes in v2:
time: 97.7 us; the launch traced here: 97.6 us
  Pallas kernels  94 us (96%)
  local copies, waits for them, and re-layouts  2.94 us (3%)
    pallas_call x1, Pallas kernels, local(): pl.pallas_call(functools.partial(kernel, shards), out_shape=(jax.ShapeDty...  94 us
    unnamed x4, local copies, waits for them, and re-layouts  2.94 us

profile of v2, /device:TPU:1, one launch (start us, length us, event | category | flops | bytes accessed | tf_op | source)
XLA Modules:
  0.0 97.6 jit_solution(8836505561941548304)
XLA Ops:
  0.6 94.0 %hyena_backward.1 = (bf16[128,2048]{1,0:T(8,128)(2,1)}, bf16[2,2,128,1024]{3,2,1,0:T(8,128)(2,1)}) custom-call(bf16[128,2048]{1,0:T(8,128)(2,1)} %x_hbm.1, bf16[128,2048]{1,0:T(8,128)(2,1)} %ct_hbm.1, bf16[2,2,128,1024]{3,2,1,0:T(8,128)(2,1)} %f_hbm.1, bf16[256,256]{1,0:T(8,128)(2,1)} %constant.12.clone.first_hbm, bf16[256,256]{1,0:T(8,128)(2,1)} %constant.13.clone.last_hbm, ...), custom_call_target="tpu_custom_call" | custom-call | tf_op jit(solution)/shard_map/hyena_backward/pallas_call | solution.py:487
  94.6 0.0 copy-start
  94.6 2.0 %copy.13 = bf16[128,2048]{1,0:T(8,128)(2,1)} copy(bf16[128,2048]{1,0:T(8,128)(2,1)} %get-tuple-element.4) | data formatting | bytes 1048576
  96.6 0.0 copy-done
  96.6 1.0 copy.14
Async XLA Ops:
  94.6 2.0 %copy-start = (bf16[2,2,128,1024]{3,2,1,0:T(8,128)(2,1)S(1)}, bf16[2,2,128,1024]{3,2,1,0:T(8,128)(2,1)}, u32[]{:S(2)}) copy-start(bf16[2,2,128,1024]{3,2,1,0:T(8,128)(2,1)} %get-tuple-element.5) | copy-start | bytes 3145732

commit v3 on v2

--- a/solution.py
+++ b/solution.py
@@ -90,8 +90,8 @@
     outer_hbm,
     twist_hbm,
     edge_hbm,
-    gi_hbm,
-    gf_hbm,
+    gi_v,
+    gf_v,
     x_v,
     f_v,
     first,
@@ -118,13 +118,10 @@
     w_low,
     back,
     y_wide,
-    gi_v,
-    gf_v,
     load_sem,
     send_sem,
     recv_sem,
     y_sem,
-    store_sem,
     plane_sem,
 ):
     width = LANES
@@ -137,6 +134,25 @@
     own = h * shards + s
     spot, column = lax.rem(s, COLUMN), lax.div(s, COLUMN)
     place = 2 * column + h
+
+    barrier = pltpu.get_barrier_semaphore()
+
+    def in_column(k):
+        return column * COLUMN + lax.rem(spot + k, COLUMN), h
+
+    def in_plane(k):
+        t = lax.rem(place + k, planes)
+        return lax.div(t, 2) * COLUMN + spot, lax.rem(t, 2)
+
+    def signal(semaphore, device):
+        pl.semaphore_signal(semaphore, inc=1, device_id=device, device_id_type=MESH)
+
+    for k in range(1, max(COLUMN, planes)):
+        far = COLUMN // 2 + (k // 2 if k % 2 else -(k // 2))
+        signal(barrier, in_column(far))
+        if k < planes:
+            far = planes // 2 + (k // 2 if k % 2 else -(k // 2))
+            signal(barrier, in_plane(far))
 
     loads = [
         pltpu.make_async_copy(source, target, load_sem.at[at])
@@ -156,23 +172,6 @@
     ]
     for load in loads:
         load.start()
-
-    barrier = pltpu.get_barrier_semaphore()
-
-    def in_column(k):
-        return column * COLUMN + lax.rem(spot + k, COLUMN), h
-
-    def in_plane(k):
-        t = lax.rem(place + k, planes)
-        return lax.div(t, 2) * COLUMN + spot, lax.rem(t, 2)
-
-    def signal(semaphore, device):
-        pl.semaphore_signal(semaphore, inc=1, device_id=device, device_id_type=MESH)
-
-    for k in range(1, COLUMN):
-        signal(barrier, in_column(k))
-    for k in range(1, planes):
-        signal(barrier, in_plane(k))
 
     def remote(phase, source, target, device, arrival=None):
         return pltpu.make_async_remote_copy(
@@ -427,8 +426,6 @@
 
     lax.fori_loop(0, shards * OWN // LANES, turn_g, 0)
 
-    store_gf = pltpu.make_async_copy(gf_v, gf_hbm, store_sem.at[0])
-    store_gf.start()
 
     def turn_y(k, missing):
         t = lax.rem(place - k + planes, planes)
@@ -439,7 +436,6 @@
         at = pl.ds(pl.multiple_of(t * LANES, LANES), LANES)
         rows = y_got[pl.ds(first_row, COLUMN)].astype(F32).reshape(LANES, width)
         gi_v[:, at] = rows.T.astype(BF16)
-        pltpu.make_async_copy(gi_v.at[:, at], gi_hbm.at[:, at], store_sem.at[1]).start()
 
     rest(planes, lambda k: turn_y(k, 0))
     turn_y(0, 1)
@@ -448,8 +444,6 @@
     whole(1, f_out, f_got, shards).wait_send()
     whole(2, g_out, g_got, shards).wait_send()
     whole(3, y_out, y_got, all_devices).wait_send()
-    store_gf.wait()
-    pltpu.make_async_copy(gi_v, gi_hbm, store_sem.at[1]).wait()
 
 
 def local(inputs, cotangent, filter_spec):
@@ -481,28 +475,25 @@
         ((OWN * shards + extra, 4 * width), BF16),
         ((OWN * shards + extra, 4 * width), F32),
         ((2, shards * OWN, width), F32),
-        ((width, channels), BF16),
-        ((2, 2, width, group), BF16),
     ]
     return pl.pallas_call(
         functools.partial(kernel, shards),
         out_shape=(
-            jax.ShapeDtypeStruct((width, channels), BF16),
-            jax.ShapeDtypeStruct((2, 2, width, group), BF16),
+            pltpu.VMEM((width, channels), BF16),
+            pltpu.VMEM((2, 2, width, group), BF16),
         ),
         in_specs=[pl.BlockSpec(memory_space=pl.ANY)] * 9,
-        out_specs=[pl.BlockSpec(memory_space=pl.ANY)] * 2,
+        out_specs=[pl.BlockSpec(memory_space=pltpu.VMEM)] * 2,
         scratch_shapes=[pltpu.VMEM(shape, dtype) for shape, dtype in scratch]
         + [
             pltpu.SemaphoreType.DMA((9,)),
             pltpu.SemaphoreType.DMA((4,)),
             pltpu.SemaphoreType.DMA((3,)),
             pltpu.SemaphoreType.DMA((2 * shards // COLUMN,)),
-            pltpu.SemaphoreType.DMA((2,)),
             pltpu.SemaphoreType.REGULAR,
         ],
         compiler_params=pltpu.CompilerParams(
-            collective_id=0, has_side_effects=True, vmem_limit_bytes=60 << 20
+            collective_id=0, has_side_effects=True, vmem_limit_bytes=58 << 20
         ),
         name="hyena_backward",
     )(inputs, cotangent, filter_spec, *constants)

time: 97.7 us -> 95.9 us (0.982)
  local copies, waits for them, and re-layouts: 2.94 us -> 1.77 us
    unnamed x4 -> x2, local copies, waits for them, and re-layouts: 2.94 us -> 1.77 us
where the time goes in v3:
time: 95.9 us; the launch traced here: 95.8 us
  Pallas kernels  93.4 us (97%)
  local copies, waits for them, and re-layouts  1.77 us (2%)
    pallas_call x1, Pallas kernels, local(): pl.pallas_call(functools.partial(kernel, shards), out_shape=(pltpu.VMEM((...  93.4 us

profile of v3, /device:TPU:1, one launch (start us, length us, event | category | flops | bytes accessed | tf_op | source)
XLA Modules:
  0.0 95.8 jit_solution(6046652935014399361)
XLA Ops:
  0.6 93.4 %hyena_backward.1 = (bf16[128,2048]{1,0:T(8,128)(2,1)S(1)}, bf16[2,2,128,1024]{3,2,1,0:T(8,128)(2,1)S(1)}) custom-call(bf16[128,2048]{1,0:T(8,128)(2,1)} %x_hbm.1, bf16[128,2048]{1,0:T(8,128)(2,1)} %ct_hbm.1, bf16[2,2,128,1024]{3,2,1,0:T(8,128)(2,1)} %f_hbm.1, bf16[256,256]{1,0:T(8,128)(2,1)} %constant.12.clone.first_hbm, ...), custom_call_target="tpu_custom_call" | custom-call | tf_op jit(solution)/shard_map/hyena_backward/pallas_call | solution.py:479
  94.0 0.8 copy.13
  94.8 1.0 %copy.14 = bf16[2,2,128,1024]{3,2,1,0:T(8,128)(2,1)} copy(bf16[2,2,128,1024]{3,2,1,0:T(8,128)(2,1)S(1)} %get-tuple-element.3) | data formatting | bytes 2097152

commit v4 on v3

--- a/solution.py
+++ b/solution.py
@@ -446,6 +446,15 @@
     whole(3, y_out, y_got, all_devices).wait_send()
 
 
+def place(gi, gf, gi_hbm, gf_hbm, sem):
+    first = pltpu.make_async_copy(gf, gf_hbm, sem.at[0])
+    second = pltpu.make_async_copy(gi, gi_hbm, sem.at[1])
+    first.start()
+    second.start()
+    first.wait()
+    second.wait()
+
+
 def local(inputs, cotangent, filter_spec):
     width, channels = inputs.shape
     shards = lax.axis_size("seq")
@@ -476,7 +485,7 @@
         ((OWN * shards + extra, 4 * width), F32),
         ((2, shards * OWN, width), F32),
     ]
-    return pl.pallas_call(
+    gradients = pl.pallas_call(
         functools.partial(kernel, shards),
         out_shape=(
             pltpu.VMEM((width, channels), BF16),
@@ -497,6 +506,17 @@
         ),
         name="hyena_backward",
     )(inputs, cotangent, filter_spec, *constants)
+    return pl.pallas_call(
+        place,
+        out_shape=(
+            pltpu.HBM((width, channels), BF16),
+            pltpu.HBM((2, 2, width, group), BF16),
+        ),
+        in_specs=[pl.BlockSpec(memory_space=pltpu.VMEM)] * 2,
+        out_specs=[pl.BlockSpec(memory_space=pl.ANY)] * 2,
+        scratch_shapes=[pltpu.SemaphoreType.DMA((2,))],
+        name="place",
+    )(*[pltpu.with_memory_space_constraint(g, pltpu.VMEM) for g in gradients])
 
 
 def solution(mesh):

time: 95.9 us -> 95.3 us (level)
  local copies, waits for them, and re-layouts: 1.77 us -> 0 us
  Pallas kernels: 93.4 us -> 94.6 us
    unnamed x2 -> x0, local copies, waits for them, and re-layouts: 1.77 us -> none
    pallas_call x0 -> x1, Pallas kernels: none -> 1.16 us  [local(): pl.pallas_call(place, out_shape=(pltpu.HBM((width, channels), BF16), pltp...]
where the time goes in v4:
time: 95.3 us; the launch traced here: 95.2 us
  Pallas kernels  94.6 us (99%)
    pallas_call x1, Pallas kernels, local(): pl.pallas_call(functools.partial(kernel, shards), out_shape=(pltpu.VMEM((...  93.4 us

profile of v4, /device:TPU:1, one launch (start us, length us, event | category | flops | bytes accessed | tf_op | source)
XLA Modules:
  0.0 95.2 jit_solution(15149967640939607224)
XLA Ops:
  0.6 93.4 %hyena_backward.1 = (bf16[128,2048]{1,0:T(8,128)(2,1)S(1)}, bf16[2,2,128,1024]{3,2,1,0:T(8,128)(2,1)S(1)}) custom-call(bf16[128,2048]{1,0:T(8,128)(2,1)} %x_hbm.1, bf16[128,2048]{1,0:T(8,128)(2,1)} %ct_hbm.1, bf16[2,2,128,1024]{3,2,1,0:T(8,128)(2,1)} %f_hbm.1, bf16[256,256]{1,0:T(8,128)(2,1)} %constant.12.clone.first_hbm, ...), custom_call_target="tpu_custom_call" | custom-call | tf_op jit(solution)/shard_map/hyena_backward/pallas_call | solution.py:488
  94.0 1.2 %place.1 = (bf16[128,2048]{1,0:T(8,128)(2,1)}, bf16[2,2,128,1024]{3,2,1,0:T(8,128)(2,1)}) custom-call(bf16[128,2048]{1,0:T(8,128)(2,1)S(1)} %get-tuple-element.4.gi, bf16[2,2,128,1024]{3,2,1,0:T(8,128)(2,1)S(1)} %get-tuple-element.5.gf), custom_call_target="tpu_custom_call" | custom-call | tf_op jit(solution)/shard_map/place/pallas_call | solution.py:509

commit v5 on v4

--- a/solution.py
+++ b/solution.py
@@ -13,6 +13,7 @@
 OWN = 8
 LANES = 128
 COLUMN = 16
+LEADS = (8, 6, 5, 3, 0, 0, 0, 0)
 F32 = jnp.float32
 BF16 = jnp.bfloat16
 
@@ -410,8 +411,33 @@
     lax.fori_loop(0, shards // 16, narrow_y, 0)
     y_got[own] = y_out[own]
     mine = h * columns + column
-    rest(planes, lambda k: to_column(3, y_out, y_got, k, 0, y_sem.at[mine]))
-    to_column(3, y_out, y_got, 0, 1, y_sem.at[mine])
+
+    def y_to(k, at):
+        t = lax.rem(place + k, planes)
+        peer_h, start = lax.rem(t, 2), lax.div(t, 2) * COLUMN
+        remote(
+            3, y_out.at[peer_h * shards + start + at], y_got.at[own], (start + at, peer_h), y_sem.at[mine]
+        ).start()
+
+    most = max(LEADS)
+
+    def send_y(step, carry):
+        for z, lead in enumerate(LEADS):
+            m = step - (most - lead)
+
+            @pl.when((m >= 0) & (m < planes))
+            def _():
+                k = lax.rem(m + 1, planes)
+                for core in range(2):
+                    at = 2 * z + core
+
+                    @pl.when((k > 0) | (spot != at))
+                    def _():
+                        y_to(k, at)
+
+        return carry
+
+    lax.fori_loop(0, planes + most, send_y, 0)
 
     whole(2, g_out, g_got, shards).wait_recv()
 

time: 95.3 us -> 94 us (0.986)
  Pallas kernels: 94.6 us -> 93.3 us
    pallas_call x1, Pallas kernels: 93.4 us -> 92.1 us  [local(): pl.pallas_call(functools.partial(kernel, shards), out_shape=(pltpu.VMEM((...]
where the time goes in v5:
time: 94 us; the launch traced here: 93.9 us
  Pallas kernels  93.3 us (99%)
    pallas_call x1, Pallas kernels, local(): pl.pallas_call(functools.partial(kernel, shards), out_shape=(pltpu.VMEM((...  92.1 us

profile of v5, /device:TPU:1, one launch (start us, length us, event | category | flops | bytes accessed | tf_op | source)
XLA Modules:
  0.0 93.9 jit_solution(2346574770152307935)
XLA Ops:
  0.6 92.1 %hyena_backward.1 = (bf16[128,2048]{1,0:T(8,128)(2,1)S(1)}, bf16[2,2,128,1024]{3,2,1,0:T(8,128)(2,1)S(1)}) custom-call(bf16[128,2048]{1,0:T(8,128)(2,1)} %x_hbm.1, bf16[128,2048]{1,0:T(8,128)(2,1)} %ct_hbm.1, bf16[2,2,128,1024]{3,2,1,0:T(8,128)(2,1)} %f_hbm.1, bf16[256,256]{1,0:T(8,128)(2,1)} %constant.12.clone.first_hbm, ...), custom_call_target="tpu_custom_call" | custom-call | tf_op jit(solution)/shard_map/hyena_backward/pallas_call | solution.py:514
  92.8 1.2 %place.1 = (bf16[128,2048]{1,0:T(8,128)(2,1)}, bf16[2,2,128,1024]{3,2,1,0:T(8,128)(2,1)}) custom-call(bf16[128,2048]{1,0:T(8,128)(2,1)S(1)} %get-tuple-element.4.gi, bf16[2,2,128,1024]{3,2,1,0:T(8,128)(2,1)S(1)} %get-tuple-element.5.gf), custom_call_target="tpu_custom_call" | custom-call | tf_op jit(solution)/shard_map/place/pallas_call | solution.py:535

commit v6 on v5

--- a/solution.py
+++ b/solution.py
@@ -500,16 +500,16 @@
         ((shards, 2, both, width), BF16),
         ((2 * shards, OWN, width), BF16),
         ((2 * shards, OWN, width), BF16),
-        ((2 * shards * both, width), F32),
+        ((2 * shards * both + both, width), F32),
         ((both * shards + both, 4 * width), BF16),
         ((both * shards + both, 4 * width), BF16),
         ((both * shards + both, 4 * width), F32),
-        ((2, shards * both, width), F32),
-        ((2, shards * both, width), F32),
+        ((2, shards * both + both, width), F32),
+        ((2, shards * both + both, width), F32),
         ((OWN * shards + extra, 4 * width), BF16),
         ((OWN * shards + extra, 4 * width), BF16),
         ((OWN * shards + extra, 4 * width), F32),
-        ((2, shards * OWN, width), F32),
+        ((2, shards * OWN + OWN, width), F32),
     ]
     gradients = pl.pallas_call(
         functools.partial(kernel, shards),

time: 94 us -> 94 us (level)
  no operation moved by 1% of the time
where the time goes in v6:
time: 94 us; the launch traced here: 93.9 us
  Pallas kernels  93.3 us (99%)
    pallas_call x1, Pallas kernels, local(): pl.pallas_call(functools.partial(kernel, shards), out_shape=(pltpu.VMEM((...  92.1 us

profile of v6, /device:TPU:1, one launch (start us, length us, event | category | flops | bytes accessed | tf_op | source)
XLA Modules:
  0.0 93.9 jit_solution(15969413714136261599)
XLA Ops:
  0.6 92.1 %hyena_backward.1 = (bf16[128,2048]{1,0:T(8,128)(2,1)S(1)}, bf16[2,2,128,1024]{3,2,1,0:T(8,128)(2,1)S(1)}) custom-call(bf16[128,2048]{1,0:T(8,128)(2,1)} %x_hbm.1, bf16[128,2048]{1,0:T(8,128)(2,1)} %ct_hbm.1, bf16[2,2,128,1024]{3,2,1,0:T(8,128)(2,1)} %f_hbm.1, bf16[256,256]{1,0:T(8,128)(2,1)} %constant.12.clone.first_hbm, ...), custom_call_target="tpu_custom_call" | custom-call | tf_op jit(solution)/shard_map/hyena_backward/pallas_call | solution.py:514
  92.8 1.2 %place.1 = (bf16[128,2048]{1,0:T(8,128)(2,1)}, bf16[2,2,128,1024]{3,2,1,0:T(8,128)(2,1)}) custom-call(bf16[128,2048]{1,0:T(8,128)(2,1)S(1)} %get-tuple-element.4.gi, bf16[2,2,128,1024]{3,2,1,0:T(8,128)(2,1)S(1)} %get-tuple-element.5.gf), custom_call_target="tpu_custom_call" | custom-call | tf_op jit(solution)/shard_map/place/pallas_call | solution.py:535

commit v7 on v6

--- a/solution.py
+++ b/solution.py
@@ -13,6 +13,7 @@
 OWN = 8
 LANES = 128
 COLUMN = 16
+TURNS = (0, 1, 15, 2, 14, 3, 13, 4, 12, 5, 11, 6, 10, 7, 9, 8)
 LEADS = (8, 6, 5, 3, 0, 0, 0, 0)
 F32 = jnp.float32
 BF16 = jnp.bfloat16
@@ -188,13 +189,13 @@
         t = lax.rem(place + k, planes)
         peer_h, start = lax.rem(t, 2), lax.div(t, 2) * COLUMN
         base = peer_h * shards + start
-        for j in range(first_spot, COLUMN):
+        for j in TURNS[first_spot:]:
             at = lax.rem(spot + j, COLUMN)
             remote(phase, out.at[base + at], got.at[own], (start + at, peer_h), arrival).start()
 
     def to_row(phase, out, got, k, first_spot):
         start = lax.rem(column + k, columns) * COLUMN
-        for j in range(first_spot, COLUMN):
+        for j in TURNS[first_spot:]:
             at = start + lax.rem(spot + j, COLUMN)
             remote(phase, out.at[at], got.at[s], (at, h)).start()
 

time: 94 us -> 94 us (level)
  no operation moved by 1% of the time
where the time goes in v7:
time: 94 us; the launch traced here: 93.9 us
  Pallas kernels  93.3 us (99%)
    pallas_call x1, Pallas kernels, local(): pl.pallas_call(functools.partial(kernel, shards), out_shape=(pltpu.VMEM((...  92.1 us

profile of v7, /device:TPU:1, one launch (start us, length us, event | category | flops | bytes accessed | tf_op | source)
XLA Modules:
  0.0 93.9 jit_solution(1886132578186608824)
XLA Ops:
  0.6 92.1 %hyena_backward.1 = (bf16[128,2048]{1,0:T(8,128)(2,1)S(1)}, bf16[2,2,128,1024]{3,2,1,0:T(8,128)(2,1)S(1)}) custom-call(bf16[128,2048]{1,0:T(8,128)(2,1)} %x_hbm.1, bf16[128,2048]{1,0:T(8,128)(2,1)} %ct_hbm.1, bf16[2,2,128,1024]{3,2,1,0:T(8,128)(2,1)} %f_hbm.1, bf16[256,256]{1,0:T(8,128)(2,1)} %constant.12.clone.first_hbm, ...), custom_call_target="tpu_custom_call" | custom-call | tf_op jit(solution)/shard_map/hyena_backward/pallas_call | solution.py:515
  92.8 1.2 %place.1 = (bf16[128,2048]{1,0:T(8,128)(2,1)}, bf16[2,2,128,1024]{3,2,1,0:T(8,128)(2,1)}) custom-call(bf16[128,2048]{1,0:T(8,128)(2,1)S(1)} %get-tuple-element.4.gi, bf16[2,2,128,1024]{3,2,1,0:T(8,128)(2,1)S(1)} %get-tuple-element.5.gf), custom_call_target="tpu_custom_call" | custom-call | tf_op jit(solution)/shard_map/place/pallas_call | solution.py:536
